TPU v7x, 32 devices: a whole 2x2x4 slice. The times are simulated.
32 devices in a mesh: group: 2 (over y), gx: 4 (over z), gz: 2 (over x), col: 2 (over core).
Axes of the slice: x: 2, y: 2, z: 4, core: 2. Of those that a mesh axis runs over, the one named last changes fastest.
Arguments:
- features: bfloat16 [32, 64, 16, 256], P(None, 'col', ('group', 'gx'), 'gz'), parts along dimension 2, may hold values from -6 to 6
- labels: int32 [64, 16, 256], P(None, ('group', 'gx'), 'gz'), parts along dimension 1, may hold values from 0 to 3
- grid_index: int32 [64], replicated, may hold values from 0 to 15
- stretch: float32 [16, 9], replicated, may hold values from 0.5 to 2
- tile_filter: float32 [32, 25], replicated, may hold values from -1.25 to 1.25
- wall_filter: float32 [32, 9], replicated, may hold values from -2 to 2
- class_weight: float32 [4, 32], replicated, may hold values from -1 to 1
Outputs:
- grad_features: bfloat16 [32, 64, 16, 256], P(None, 'col', ('group', 'gx'), 'gz'), parts along dimension 2
- grad_tile_filter: float32 [64, 25], P('group'), parts along dimension 0
- grad_wall_filter: float32 [64, 9], P('group'), parts along dimension 0
- grad_class_weight: float32 [8, 32], P('group'), parts along dimension 0
There are 2 independent parts, one for each index of `group`. A program takes and returns all parts, laid end to end along the dimension named above; an argument that names none is the same for every part. Nothing has to cross between parts.
All inputs are finite; a program needn't handle non-finite values.
Results may differ from a plain program's by a relative error of at most 0.0064.
Values may be sent and summed in bfloat16 or wider, within the bound.
A program may use at most 64 MiB of HBM per device.

v0:
```python
import jax
import jax.numpy as jnp
from jax import lax
from jax.sharding import PartitionSpec as P


def with_halo(value, sides, width):
    for axis, dim in sides:
        size, length = (lax.axis_size(axis), value.shape[dim])
        up = [(i, (i + 1) % size) for i in range(size)]
        down = [(j, i) for i, j in up]
        last = lax.slice_in_dim(value, length - width, length, axis=dim)
        leading = lax.slice_in_dim(value, 0, width, axis=dim)
        before = lax.ppermute(last, axis, up)
        after = lax.ppermute(leading, axis, down)
        value = jnp.concatenate([before, value, after], axis=dim)
    return value


def rim_tiles(field):
    return with_halo(field, (("gx", 2), ("gz", 3)), 2)


def band_table(grid_index, stretch):
    levels = stretch.shape[0]
    onehot = (grid_index[:, None] == jnp.arange(levels, dtype=jnp.int32)[None, :]).astype(
        jnp.float32
    )
    return jnp.dot(onehot, stretch, precision=lax.Precision.HIGHEST)


def wall_forward(smooth_ext, wall_rows, band_rows):
    rows = band_rows.shape[0]
    total = jnp.zeros((smooth_ext.shape[0], rows) + smooth_ext.shape[2:], jnp.float32)
    for k in range(9):
        tap = wall_rows[:, k][:, None] * band_rows[:, k][None, :]
        total = total + tap[:, :, None, None] * smooth_ext[:, k : k + rows].astype(jnp.float32)
    return total


def wall_backward(grad_ext, wall_rows, band_ext, rows):
    total = jnp.zeros((grad_ext.shape[0], rows) + grad_ext.shape[2:], jnp.float32)
    for k in range(9):
        first = 8 - k
        tap = wall_rows[:, k][:, None] * band_ext[first : first + rows, k][None, :]
        total = total + tap[:, :, None, None] * grad_ext[:, first : first + rows].astype(
            jnp.float32
        )
    return total


def shards(features, labels, grid_index, stretch, tile_filter, wall_filter, class_weight):
    chans, half_rows, cells_x, cells_z = features.shape
    all_rows = labels.shape[0]
    classes = class_weight.shape[0]
    volume = all_rows * cells_x * lax.axis_size("gx") * cells_z * lax.axis_size("gz")
    widened = rim_tiles(features)
    smooth = jnp.zeros(features.shape, jnp.float32)
    for i in range(5):
        for j in range(5):
            weight = tile_filter[:, 5 * i + j][:, None, None, None]
            smooth = smooth + weight * widened[:, :, i : i + cells_x, j : j + cells_z].astype(
                jnp.float32
            )
    smoothed = smooth.astype(jnp.bfloat16)
    bands = band_table(grid_index, stretch)
    bands_pad = jnp.pad(bands, ((4, 4), (0, 0)))
    place = lax.axis_index("col")
    share = chans // lax.axis_size("col")
    first_chan = place * share
    pencil = lax.all_to_all(smoothed, "col", split_axis=0, concat_axis=1, tiled=True)
    smooth_ext = jnp.pad(pencil, ((0, 0), (4, 4), (0, 0), (0, 0)))
    wall_rows = lax.dynamic_slice_in_dim(wall_filter, first_chan, share, 0)
    class_rows = lax.dynamic_slice_in_dim(class_weight, first_chan, share, 1)
    wall_out = wall_forward(smooth_ext, wall_rows, bands)
    sig = jax.nn.sigmoid(wall_out)
    hidden = wall_out * sig
    partial_scores = jnp.einsum(
        "kc,cyxz->kyxz", class_rows, hidden, precision=lax.Precision.HIGHEST
    )
    scores = lax.psum(partial_scores, "col")
    targets = (labels[None] == jnp.arange(classes, dtype=jnp.int32)[:, None, None, None]).astype(
        jnp.float32
    )
    errors = scores - targets
    grad_hidden = jnp.einsum("kc,kyxz->cyxz", class_rows, errors, precision=lax.Precision.HIGHEST)
    grad_wall = (grad_hidden * sig * (1.0 + wall_out * (1.0 - sig))).astype(jnp.bfloat16)
    class_part = jnp.einsum("kyxz,cyxz->kc", errors, hidden, precision=lax.Precision.HIGHEST)
    grad_vals = grad_wall.astype(jnp.float32)
    wall_part = jnp.stack(
        [
            jnp.sum(
                grad_vals
                * bands[:, k][None, :, None, None]
                * smooth_ext[:, k : k + all_rows].astype(jnp.float32),
                axis=(1, 2, 3),
            )
            for k in range(9)
        ],
        axis=1,
    )
    grad_ext = jnp.pad(grad_wall, ((0, 0), (4, 4), (0, 0), (0, 0)))
    grad_smooth = wall_backward(grad_ext, wall_rows, bands_pad, all_rows).astype(jnp.bfloat16)
    grad_tile = lax.all_to_all(grad_smooth, "col", split_axis=1, concat_axis=0, tiled=True)
    wall_full = lax.dynamic_update_slice_in_dim(
        jnp.zeros((chans, 9), jnp.float32), wall_part, first_chan, 0
    )
    class_full = lax.dynamic_update_slice_in_dim(
        jnp.zeros((classes, chans), jnp.float32), class_part, first_chan, 1
    )
    grad_widened = rim_tiles(grad_tile)
    grad_tile_vals = grad_tile.astype(jnp.float32)
    grad_field = jnp.zeros(features.shape, jnp.float32)
    tile_terms = []
    for i in range(5):
        for j in range(5):
            weight = tile_filter[:, 5 * i + j][:, None, None, None]
            grad_field = grad_field + weight * grad_widened[
                :, :, 4 - i : 4 - i + cells_x, 4 - j : 4 - j + cells_z
            ].astype(jnp.float32)
            shifted = widened[:, :, i : i + cells_x, j : j + cells_z].astype(jnp.float32)
            tile_terms.append(jnp.sum(shifted * grad_tile_vals, axis=(1, 2, 3)))
    tile_part = jnp.stack(tile_terms, axis=1)
    totals = lax.psum((tile_part, wall_full, class_full), ("gx", "gz", "col"))
    return (
        grad_field.astype(jnp.bfloat16),
        totals[0] / volume,
        totals[1] / volume,
        totals[2] / volume,
    )


def solution(mesh):
    return jax.shard_map(
        shards,
        mesh=mesh,
        in_specs=(
            P(None, "col", ("group", "gx"), "gz"),
            P(None, ("group", "gx"), "gz"),
            P(),
            P(),
            P(),
            P(),
            P(),
        ),
        out_specs=(
            P(None, "col", ("group", "gx"), "gz"),
            P("group", None),
            P("group", None),
            P("group", None),
        ),
        check_vma=False,
    )
```

profile of v0, /device:TPU:0, one launch (start us, length us, event | category | flops | bytes accessed | tf_op | source)
XLA Modules:
  0.0 227.5 jit_solution(17064217156550470900)
XLA Ops:
  7.2 1.1 copy.53
  8.4 3.1 %collective-permute-start = (bf16[32,32,2,128]{3,1,2,0:T(8,128)(2,1)S(1)}, bf16[32,32,2,128]{3,1,2,0:T(8,128)(2,1)S(1)}, u32[]{:S(2)}, u32[]{:S(2)}) collective-permute-start(bf16[32,32,2,128]{3,1,2,0:T(8,128)(2,1)S(1)} %copy.53), channel_id=1, source_target_pairs={{0,4},{4,8},{8,12},{12,0},{1,5},{5,9},{9,13},{13,1},{2,6},{6,10},{... | collective-permute-start | bytes 1572872 | tf_op jit(solution)/shard_map/ppermute | solution.py:14
  11.5 2.1 collective-permute-start.1
  13.6 0.8 fusion.110
  14.6 1.1 dynamic-slice_bitcast_fusion.8
  15.7 0.7 broadcast_multiply_fusion.4
  16.4 0.7 broadcast_multiply_fusion.2
  17.1 0.7 broadcast_multiply_fusion
  18.1 2.5 %slice_reduce_fusion.24 = (f32[32]{0:T(128)S(1)}, f32[32]{0:T(128)S(1)}, f32[32]{0:T(128)S(1)}, f32[32]{0:T(128)S(1)}, f32[32]{0:T(128)S(1)}, /*index=5*/f32[32]...) fusion(f32[32,25]{1,0:T(8,128)} %param.11), kind=kLoop, calls=%fused_computation.296 | loop fusion | bytes 4864 | tf_op jit(solution)/shard_map/slice | solution.py:117
  20.6 5.7 %collective-permute-done = bf16[32,32,2,128]{3,1,2,0:T(8,128)(2,1)S(1)} collective-permute-done((bf16[32,32,2,128]{3,1,2,0:T(8,128)(2,1)S(1)}, bf16[32,32,2,128]{3,1,2,0:T(8,128)(2,1)S(1)}, u32[]{:S(2)}, u32[]{:S(2)}) %collective-permute-start) | collective-permute-done | bytes 524320 | tf_op jit(solution)/shard_map/ppermute | solution.py:14
  26.3 1.4 constant_dynamic-update-slice_fusion.1
  27.7 8.4 %collective-permute-done.1 = bf16[32,32,2,128]{3,1,2,0:T(8,128)(2,1)S(1)} collective-permute-done((bf16[32,32,2,128]{3,1,2,0:T(8,128)(2,1)S(1)}, bf16[32,32,2,128]{3,1,2,0:T(8,128)(2,1)S(1)}, u32[]{:S(2)}, u32[]{:S(2)}) %collective-permute-start.1) | collective-permute-done | bytes 524320 | tf_op jit(solution)/shard_map/ppermute | solution.py:15
  36.1 0.8 copy-done.9
  37.0 1.9 fusion.129
  38.9 3.1 %copy.56 = bf16[32,32,6,2]{1,0,3,2:T(8,128)(2,1)} copy(bf16[32,32,6,2]{3,1,2,0:T(8,128)(2,1)} %get-tuple-element.96) | data formatting | bytes 49152 | tf_op jit(solution)/shard_map/slice | solution.py:12
  42.0 1.5 collective-permute-start.2
  43.5 2.1 copy.58
  46.2 0.8 slice_reduce_fusion.23
  47.0 2.2 copy.57
  49.2 1.4 collective-permute-done.3
  50.6 3.0 %copy.59 = bf16[32,32,6,2]{3,1,2,0:T(8,128)(2,1)} copy(bf16[32,32,6,2]{1,0,3,2:T(8,128)(2,1)} %collective-permute-done.3) | data formatting | bytes 49152 | tf_op jit(solution)/shard_map/ppermute | solution.py:15
  53.5 11.2 %fusion.90 = (bf16[32,32,2,128]{3,1,2,0:T(8,128)(2,1)S(1)}, bf16[32,32,2,128]{3,1,2,0:T(8,128)(2,1)}, bf16[32,32,2,128]{3,1,2,0:T(8,128)(2,1)}) fusion(bf16[32,32,2,128]{3,1,2,0:T(8,128)(2,1)} %copy-done.9, bf16[32,32,2,128]{3,1,2,0:T(8,128)(2,1)} %copy-done.5, bf16[32,32,2,128]{3,1,2,0:T(8,128)(2,1)} %copy-done.7, f32[32]{0:T(128)} %get-tuple-element.81, ...), kind=kLoop, calls=%fused_computation.211 | loop fusion | flops 37486592 | bytes 4770944 | tf_op jit(solution)/shard_map/convert_element_type | solution.py:65
  64.8 4.2 %all_to_all.36 = bf16[32,32,2,128]{3,1,2,0:T(8,128)(2,1)S(1)} all-to-all(bf16[32,32,2,128]{3,1,2,0:T(8,128)(2,1)S(1)} %get-tuple-element.88), channel_id=1, replica_groups=mesh['group'=2,'gx'=4,'gz'=2,'col'=2] {'col'}, dimensions={0} | all-to-all | bytes 1048576 | tf_op jit(solution)/shard_map/all_to_all | solution.py:71
  69.2 2.7 %fusion.88 = (f32[16,64,2,128]{3,0,2,1:T(8,128)S(1)}, f32[16,64,2,128]{3,0,2,1:T(8,128)}) fusion(f32[16,64]{0,1:T(8,128)S(1)} %get-tuple-element.138, f32[16,64]{0,1:T(8,128)S(1)} %get-tuple-element.140, f32[16,64]{0,1:T(8,128)S(1)} %get-tuple-element.134, f32[16,64]{0,1:T(8,128)S(1)} %get-tuple-element.142, bf16[16,64,2,128]{3,0,2,1:T(8,128)(2,1)S(1)} %bitcast.143, ...), kind=kLoop, calls=%fused_computation.209 | loop fusion | flops 7864320 | bytes 2658304 | tf_op jit(solution)/shard_map/mul | solution.py:77
  72.0 1.3 fusion.113
  73.4 18.9 %all-reduce.6.cloned.1.call-done = f32[4,64,2,128]{3,0,2,1:T(4,128)} async-done(((f32[4,64,2,128]{3,0,2,1:T(4,128)}), f32[4,64,2,128]{3,0,2,1:T(4,128)}) %all-reduce.6.cloned.1.call-update) | async-done | bytes 262160 | tf_op jit(solution)/shard_map/psum | solution.py:81
  92.3 4.8 %fusion.42 = (f32[16]{0:T(128)S(1)}, f32[16]{0:T(128)S(1)}, f32[16]{0:T(128)S(1)}, f32[16]{0:T(128)S(1)}, f32[16]{0:T(128)S(1)}, /*index=5*/f32[16]{0:T(128)S(1)...) fusion(f32[64]{0:T(128)} %copy-done.40, ...), kind=kOutput, calls=%fused_computation.162 | convolution fusion | flops 24838000 | bytes 2952516 | tf_op jit(solution)/shard_map/kc,kyxz->cyxz/dot_general | solution.py:86
  97.2 1.7 fusion.48
  99.0 4.3 %all_to_all.37 = bf16[16,64,2,128]{3,0,2,1:T(8,128)(2,1)S(1)} all-to-all(bf16[16,64,2,128]{3,0,2,1:T(8,128)(2,1)S(1)} %fusion.48), channel_id=1, replica_groups=mesh['group'=2,'gx'=4,'gz'=2,'col'=2] {'col'}, dimensions={1} | all-to-all | bytes 1048576 | tf_op jit(solution)/shard_map/all_to_all | solution.py:104
  103.5 3.9 %fusion.85 = (f32[32]{0:T(128)S(1)}, f32[32]{0:T(128)S(1)}, f32[32]{0:T(128)S(1)}, f32[32]{0:T(128)S(1)}, f32[32]{0:T(128)S(1)}, /*index=5*/f32[32]{0:T(128)S(1)}, f32[32]{0:T(128)S(1)}, f32[32]{0:T(128)S(1)}, f32[32]{0:T(128)S(1)}) fusion(bf16[2,16,32,2,128]{4,2,3,1,0:T(8,128)(2,1)S(1)} %copy.64, bf16[32,32,6,2]{3,1,2,0:T(8,128)(2,1)S(1)} %copy-done.3, ...), kind=kLoop, calls=%fused_computation.205 | loop fusion | flops 14417632 | bytes 2122880 | tf_op jit(solution)/shard_map/reduce_sum | solution.py:122
  107.5 3.8 %fusion.82 = (f32[32]{0:T(128)S(1)}, f32[32]{0:T(128)S(1)}, f32[32]{0:T(128)S(1)}, f32[32]{0:T(128)S(1)}, f32[32]{0:T(128)S(1)}, /*index=5*/f32[32]{0:T(128)S(1)}, f32[32]{0:T(128)S(1)}, f32[32]{0:T(128)S(1)}, f32[32]{0:T(128)S(1)}) fusion(bf16[2,16,32,2,128]{4,2,3,1,0:T(8,128)(2,1)S(1)} %copy.64, ...), kind=kLoop, calls=%fused_computation.202 | loop fusion | flops 14417632 | bytes 2122880 | tf_op jit(solution)/shard_map/reduce_sum | solution.py:122
  111.2 1.8 collective-permute-start.4
  113.0 2.1 collective-permute-start.5
  115.1 1.1 fusion.84
  116.2 1.4 convolution_bitcast_fusion
  118.2 72.8 %all-reduce.3 = (f32[32,25]{0,1:T(8,128)S(1)}, f32[32,9]{0,1:T(8,128)S(1)}, f32[4,32]{1,0:T(4,128)S(1)}) all-reduce(f32[32,25]{0,1:T(8,128)S(1)} %stack.133, f32[32,9]{0,1:T(8,128)S(1)} %dynamic_update_slice.6, f32[4,32]{1,0:T(4,128)S(1)} %dynamic_update_slice.7), channel_id=1, replica_groups=mesh['group'=2,'gx'=4,'gz'=2,'col'=2] {'gx','gz','col'}, use_global_device_ids=true, to_apply=%region_26.27 | all-reduce | flops 1216 | bytes 9728 | tf_op jit(solution)/shard_map/psum | solution.py:124
  191.6 0.8 copy-done.12
  192.4 1.4 pad_maximum_fusion.1
  193.7 2.4 %fusion.128 = (bf16[32,32,6,2]{3,1,2,0:T(8,128)(2,1)}, bf16[32,32,6,2]{3,1,2,0:T(8,128)(2,1)}) fusion(bf16[32,32,6,128]{3,1,2,0:T(8,128)(2,1)S(1)} %pad_maximum_fusion.1), kind=kLoop, calls=%fused_computation.344 | loop fusion | bytes 98304 | tf_op jit(solution)/shard_map/slice | solution.py:13
  196.2 2.6 %copy.75 = bf16[32,32,6,2]{1,0,3,2:T(8,128)(2,1)S(1)} copy(bf16[32,32,6,2]{3,1,2,0:T(8,128)(2,1)} %get-tuple-element.93) | data formatting | bytes 49152
  198.8 2.5 %copy.76 = bf16[32,32,6,2]{1,0,3,2:T(8,128)(2,1)S(1)} copy(bf16[32,32,6,2]{3,1,2,0:T(8,128)(2,1)} %get-tuple-element.94) | data formatting | bytes 49152
  201.4 2.1 collective-permute-start.7
  204.0 0.7 copy.72
  204.7 1.4 copy.66
  206.1 2.2 copy.68
  208.5 4.3 %pad_maximum_fusion = (bf16[32,32,6,130]{3,1,2,0:T(8,128)(2,1)S(1)}, bf16[32,32,6,130]{3,1,2,0:T(8,128)(2,1)S(1)}) fusion(bf16[32,32,6,2]{3,1,2,0:T(8,128)(2,1)S(1)} %copy.66, bf16[32,32,2,128]{3,1,2,0:T(8,128)(2,1)} %collective-permute-done.5, bf16[32,32,2,128]{3,1,2,0:T(8,128)(2,1)S(1)} %bitcast.139, bf16[32,32,2,128]{3,1,2,0:T(8,128)(2,1)S(1)} %copy-done.13, ...), kind=kLoop, calls=%fused_computation.72 | loop fusion | flops 12779520 | bytes 4816896 | tf_op jit(solution)/shard_map/concatenate | solution.py:16
  212.9 6.4 %fusion.89 = bf16[32,32,2,128]{3,1,2,0:T(8,128)(2,1)S(1)} fusion(bf16[32,32,2,128]{3,1,2,0:T(8,128)(2,1)S(1)} %copy-done.13, bf16[32,32,2,128]{3,1,2,0:T(8,128)(2,1)S(1)} %bitcast.140, bf16[32,32,2,128]{3,1,2,0:T(8,128)(2,1)} %collective-permute-done.5, bf16[32,32,6,130]{3,1,2,0:T(8,128)(2,1)S(1)} %get-tuple-element.92, ...), kind=kLoop, calls=%fused_computation.210 | loop fusion | flops 20185088 | bytes 12586112 | tf_op jit(solution)/shard_map/convert_element_type | solution.py:126
  219.3 1.3 copy.71
  (121 shorter events, 3.5 us)
Async XLA Ops:
  7.2 6.4 %copy-start = (f32[16,9]{1,0:T(8,128)S(1)}, f32[16,9]{1,0:T(8,128)}, u32[]{:S(2)}) copy-start(f32[16,9]{1,0:T(8,128)} %param.10) | copy-start | bytes 1732
  7.2 85.1 %all-reduce.6.cloned.1.call-start = ((), (), s32[]{:S(2)}) async-start(), calls=%async_computation.2 | async-start | bytes 524288 | tf_op jit(solution)/shard_map/psum | solution.py:81
  8.4 27.7 %copy-start.5 = (bf16[32,32,2,128]{3,1,2,0:T(8,128)(2,1)}, bf16[32,32,2,128]{3,1,2,0:T(8,128)(2,1)S(1)}, u32[]{:S(2)}) copy-start(bf16[32,32,2,128]{3,1,2,0:T(8,128)(2,1)S(1)} %copy.53) | copy-start | bytes 1572868
  8.4 17.9 %collective-permute-start = (bf16[32,32,2,128]{3,1,2,0:T(8,128)(2,1)S(1)}, bf16[32,32,2,128]{3,1,2,0:T(8,128)(2,1)S(1)}, u32[]{:S(2)}, u32[]{:S(2)}) collective-permute-start(bf16[32,32,2,128]{3,1,2,0:T(8,128)(2,1)S(1)} %copy.53), channel_id=1, source_target_pairs={{0,4},{4,8},{8,12},{12,0},{1,5},{5,9},{9,13},{13,1},{2,6},{6,10},{... | collective-permute-start | bytes 1572872 | tf_op jit(solution)/shard_map/ppermute | solution.py:14
  11.5 24.6 %collective-permute-start.1 = (bf16[32,32,2,128]{3,1,2,0:T(8,128)(2,1)S(1)}, bf16[32,32,2,128]{3,1,2,0:T(8,128)(2,1)S(1)}, u32[]{:S(2)}, u32[]{:S(2)}) collective-permute-start(bf16[32,32,2,128]{3,1,2,0:T(8,128)(2,1)S(1)} %copy.53), channel_id=1, source_target_pairs={{4,0},{8,4},{12,8},{0,12},{5,1},{9,5},{13,9},{1,13},{6,2},{10,6},{... | collective-permute-start | bytes 1572872 | tf_op jit(solution)/shard_map/ppermute | solution.py:15
  14.6 6.0 %copy-start.48 = (f32[64]{0:T(128)}, f32[64]{0:T(128)S(1)}, u32[]{:S(2)}) copy-start(f32[64]{0:T(128)S(1)} %get-tuple-element.113) | copy-start | bytes 772
  26.3 9.8 %copy-start.7 = (bf16[32,32,2,128]{3,1,2,0:T(8,128)(2,1)}, bf16[32,32,2,128]{3,1,2,0:T(8,128)(2,1)S(1)}, u32[]{:S(2)}) copy-start(bf16[32,32,2,128]{3,1,2,0:T(8,128)(2,1)S(1)} %collective-permute-done) | copy-start | bytes 1572868
  38.9 7.3 %copy-start.4 = (f32[32,25]{1,0:T(8,128)S(1)}, f32[32,25]{1,0:T(8,128)}, u32[]{:S(2)}) copy-start(f32[32,25]{1,0:T(8,128)} %param.11) | copy-start | bytes 9604
  42.0 5.0 %collective-permute-start.2 = (bf16[32,32,6,2]{1,0,3,2:T(8,128)(2,1)}, bf16[32,32,6,2]{1,0,3,2:T(8,128)(2,1)}, u32[]{:S(2)}, u32[]{:S(2)}) collective-permute-start(bf16[32,32,6,2]{1,0,3,2:T(8,128)(2,1)} %copy.56), channel_id=1, source_target_pairs={{0,2},{2,0},{1,3},{3,1},{4,6},{6,4},{5,7},{7,5},{8,10},{10,8},{9,1... | collective-permute-start | bytes 73736 | tf_op jit(solution)/shard_map/ppermute | solution.py:14
  45.6 4.9 %collective-permute-start.3 = (bf16[32,32,6,2]{1,0,3,2:T(8,128)(2,1)}, bf16[32,32,6,2]{1,0,3,2:T(8,128)(2,1)}, u32[]{:S(2)}, u32[]{:S(2)}) collective-permute-start(bf16[32,32,6,2]{1,0,3,2:T(8,128)(2,1)} %copy.58), channel_id=1, source_target_pairs={{2,0},{0,2},{3,1},{1,3},{6,4},{4,6},{7,5},{5,7},{10,8},{8,10},{11,... | collective-permute-start | bytes 73736 | tf_op jit(solution)/shard_map/ppermute | solution.py:15
  49.2 15.6 %copy-start.1 = (bf16[32,32,6,2]{3,1,2,0:T(8,128)(2,1)}, bf16[32,32,6,2]{3,1,2,0:T(8,128)(2,1)S(1)}, u32[]{:S(2)}) copy-start(bf16[32,32,6,2]{3,1,2,0:T(8,128)(2,1)S(1)} %copy.57) | copy-start | bytes 73732
  64.7 7.2 %copy-start.39 = (f32[4,32]{1,0:T(4,128)S(1)}, f32[4,32]{1,0:T(4,128)}, u32[]{:S(2)}) copy-start(f32[4,32]{1,0:T(4,128)} %param.13) | copy-start | bytes 1540
  92.3 4.9 %copy-start.17 = (f32[16,64]{0,1:T(8,128)S(1)}, f32[16,64]{0,1:T(8,128)}, u32[]{:S(2)}) copy-start(f32[16,64]{0,1:T(8,128)} %get-tuple-element.129) | copy-start | bytes 12292
  92.3 4.9 %copy-start.18 = (f32[16,64]{0,1:T(8,128)S(1)}, f32[16,64]{0,1:T(8,128)}, u32[]{:S(2)}) copy-start(f32[16,64]{0,1:T(8,128)} %get-tuple-element.145) | copy-start | bytes 12292
  92.3 4.9 %copy-start.19 = (f32[16,64]{0,1:T(8,128)S(1)}, f32[16,64]{0,1:T(8,128)}, u32[]{:S(2)}) copy-start(f32[16,64]{0,1:T(8,128)} %get-tuple-element.133) | copy-start | bytes 12292
  92.3 4.9 %copy-start.20 = (f32[16,64]{0,1:T(8,128)S(1)}, f32[16,64]{0,1:T(8,128)}, u32[]{:S(2)}) copy-start(f32[16,64]{0,1:T(8,128)} %get-tuple-element.143) | copy-start | bytes 12292
  92.3 4.9 %copy-start.21 = (f32[16,64]{0,1:T(8,128)S(1)}, f32[16,64]{0,1:T(8,128)}, u32[]{:S(2)}) copy-start(f32[16,64]{0,1:T(8,128)} %get-tuple-element.137) | copy-start | bytes 12292
  92.3 4.9 %copy-start.22 = (f32[16,64]{0,1:T(8,128)S(1)}, f32[16,64]{0,1:T(8,128)}, u32[]{:S(2)}) copy-start(f32[16,64]{0,1:T(8,128)} %get-tuple-element.141) | copy-start | bytes 12292
  97.1 6.3 %copy-start.3 = (bf16[32,32,6,2]{3,1,2,0:T(8,128)(2,1)S(1)}, bf16[32,32,6,2]{3,1,2,0:T(8,128)(2,1)}, u32[]{:S(2)}) copy-start(bf16[32,32,6,2]{3,1,2,0:T(8,128)(2,1)} %copy.59) | copy-start | bytes 73732
  98.9 8.5 %copy-start.2 = (bf16[32,32,6,2]{3,1,2,0:T(8,128)(2,1)S(1)}, bf16[32,32,6,2]{3,1,2,0:T(8,128)(2,1)}, u32[]{:S(2)}) copy-start(bf16[32,32,6,2]{3,1,2,0:T(8,128)(2,1)} %copy-done.1) | copy-start | bytes 73732
  103.5 11.6 %copy-start.6 = (bf16[32,32,2,128]{3,1,2,0:T(8,128)(2,1)S(1)}, bf16[32,32,2,128]{3,1,2,0:T(8,128)(2,1)}, u32[]{:S(2)}) copy-start(bf16[32,32,2,128]{3,1,2,0:T(8,128)(2,1)} %copy-done.5) | copy-start | bytes 1572868
  103.5 11.6 %copy-start.8 = (bf16[32,32,2,128]{3,1,2,0:T(8,128)(2,1)S(1)}, bf16[32,32,2,128]{3,1,2,0:T(8,128)(2,1)}, u32[]{:S(2)}) copy-start(bf16[32,32,2,128]{3,1,2,0:T(8,128)(2,1)} %copy-done.7) | copy-start | bytes 1572868
  103.5 11.6 %copy-start.10 = (bf16[32,32,2,128]{3,1,2,0:T(8,128)(2,1)S(1)}, bf16[32,32,2,128]{3,1,2,0:T(8,128)(2,1)}, u32[]{:S(2)}) copy-start(bf16[32,32,2,128]{3,1,2,0:T(8,128)(2,1)} %copy-done.9) | copy-start | bytes 1572868
  103.5 11.6 %copy-start.11 = (bf16[32,32,2,128]{3,2,1,0:T(2,128)(2,1)S(1)}, bf16[32,32,2,128]{3,2,1,0:T(2,128)(2,1)}, u32[]{:S(2)}) copy-start(bf16[32,32,2,128]{3,2,1,0:T(2,128)(2,1)} %param.7) | copy-start | bytes 1572868
  103.5 11.6 %copy-start.14 = (bf16[32,32,2,128]{3,1,2,0:T(8,128)(2,1)S(1)}, bf16[32,32,2,128]{3,1,2,0:T(8,128)(2,1)}, u32[]{:S(2)}) copy-start(bf16[32,32,2,128]{3,1,2,0:T(8,128)(2,1)} %get-tuple-element.89) | copy-start | bytes 1572868
  103.5 11.6 %copy-start.15 = (bf16[32,32,2,128]{3,1,2,0:T(8,128)(2,1)S(1)}, bf16[32,32,2,128]{3,1,2,0:T(8,128)(2,1)}, u32[]{:S(2)}) copy-start(bf16[32,32,2,128]{3,1,2,0:T(8,128)(2,1)} %get-tuple-element.90) | copy-start | bytes 1572868
  107.4 8.8 %copy-start.16 = (f32[4,64,2,128]{3,0,2,1:T(4,128)S(1)}, f32[4,64,2,128]{3,0,2,1:T(4,128)}, u32[]{:S(2)}) copy-start(f32[4,64,2,128]{3,0,2,1:T(4,128)} %all-reduce.6.cloned.1.call-done) | copy-start | bytes 786436
  107.4 8.8 %copy-start.23 = (s32[64,2,128]{2,1,0:T(2,128)S(1)}, s32[64,2,128]{2,1,0:T(2,128)}, u32[]{:S(2)}) copy-start(s32[64,2,128]{2,1,0:T(2,128)} %param.8) | copy-start | bytes 196612
  111.2 80.3 %collective-permute-start.4 = (bf16[32,32,2,128]{3,1,2,0:T(8,128)(2,1)S(1)}, bf16[32,32,2,128]{3,1,2,0:T(8,128)(2,1)S(1)}, u32[]{:S(2)}, u32[]{:S(2)}) collective-permute-start(bf16[32,32,2,128]{3,1,2,0:T(8,128)(2,1)S(1)} %bitcast.136), channel_id=1, source_target_pairs={{0,4},{4,8},{8,12},{12,0},{1,5},{5,9},{9,13},{13,1},{2,6},{6,10},{... | collective-permute-start | bytes 1572872 | tf_op jit(solution)/shard_map/ppermute | solution.py:14
  113.0 79.4 %collective-permute-start.5 = (bf16[32,32,2,128]{3,1,2,0:T(8,128)(2,1)S(1)}, bf16[32,32,2,128]{3,1,2,0:T(8,128)(2,1)}, u32[]{:S(2)}, u32[]{:S(2)}) collective-permute-start(bf16[32,32,2,128]{3,1,2,0:T(8,128)(2,1)S(1)} %bitcast.137), channel_id=1, source_target_pairs={{4,0},{8,4},{12,8},{0,12},{5,1},{9,5},{13,9},{1,13},{6,2},{10,6},{... | collective-permute-start | bytes 1572872 | tf_op jit(solution)/shard_map/ppermute | solution.py:15
  196.2 12.2 %copy-start.13 = (bf16[32,32,2,128]{3,1,2,0:T(8,128)(2,1)S(1)}, bf16[32,32,2,128]{3,1,2,0:T(8,128)(2,1)}, u32[]{:S(2)}) copy-start(bf16[32,32,2,128]{3,1,2,0:T(8,128)(2,1)} %copy-done.12) | copy-start | bytes 1572868
  198.8 6.0 %collective-permute-start.6 = (bf16[32,32,6,2]{1,0,3,2:T(8,128)(2,1)S(1)}, bf16[32,32,6,2]{1,0,3,2:T(8,128)(2,1)S(1)}, u32[]{:S(2)}, u32[]{:S(2)}) collective-permute-start(bf16[32,32,6,2]{1,0,3,2:T(8,128)(2,1)S(1)} %copy.75), channel_id=1, source_target_pairs={{2,0},{0,2},{3,1},{1,3},{6,4},{4,6},{7,5},{5,7},{10,8},{8,10},{11,... | collective-permute-start | bytes 73736 | tf_op jit(solution)/shard_map/ppermute | solution.py:15
  201.4 4.7 %collective-permute-start.7 = (bf16[32,32,6,2]{1,0,3,2:T(8,128)(2,1)S(1)}, bf16[32,32,6,2]{1,0,3,2:T(8,128)(2,1)S(1)}, u32[]{:S(2)}, u32[]{:S(2)}) collective-permute-start(bf16[32,32,6,2]{1,0,3,2:T(8,128)(2,1)S(1)} %copy.76), channel_id=1, source_target_pairs={{0,2},{2,0},{1,3},{3,1},{4,6},{6,4},{5,7},{7,5},{8,10},{10,8},{9,1... | collective-permute-start | bytes 73736 | tf_op jit(solution)/shard_map/ppermute | solution.py:14
  208.3 4.4 %copy-start.24 = (f32[32]{0:T(128)S(1)}, f32[32]{0:T(128)}, u32[]{:S(2)}) copy-start(f32[32]{0:T(128)} %get-tuple-element.64) | copy-start | bytes 388
  208.3 4.4 %copy-start.25 = (f32[32]{0:T(128)S(1)}, f32[32]{0:T(128)}, u32[]{:S(2)}) copy-start(f32[32]{0:T(128)} %get-tuple-element.65) | copy-start | bytes 388
  208.3 4.4 %copy-start.26 = (f32[32]{0:T(128)S(1)}, f32[32]{0:T(128)}, u32[]{:S(2)}) copy-start(f32[32]{0:T(128)} %get-tuple-element.66) | copy-start | bytes 388
  208.3 4.4 %copy-start.27 = (f32[32]{0:T(128)S(1)}, f32[32]{0:T(128)}, u32[]{:S(2)}) copy-start(f32[32]{0:T(128)} %get-tuple-element.67) | copy-start | bytes 388
  208.4 4.4 %copy-start.28 = (f32[32]{0:T(128)S(1)}, f32[32]{0:T(128)}, u32[]{:S(2)}) copy-start(f32[32]{0:T(128)} %get-tuple-element.68) | copy-start | bytes 388
  208.4 4.4 %copy-start.29 = (f32[32]{0:T(128)S(1)}, f32[32]{0:T(128)}, u32[]{:S(2)}) copy-start(f32[32]{0:T(128)} %get-tuple-element.69) | copy-start | bytes 388
  208.4 4.4 %copy-start.30 = (f32[32]{0:T(128)S(1)}, f32[32]{0:T(128)}, u32[]{:S(2)}) copy-start(f32[32]{0:T(128)} %get-tuple-element.70) | copy-start | bytes 388
  208.4 4.4 %copy-start.31 = (f32[32]{0:T(128)S(1)}, f32[32]{0:T(128)}, u32[]{:S(2)}) copy-start(f32[32]{0:T(128)} %get-tuple-element.71) | copy-start | bytes 388
  208.4 4.4 %copy-start.32 = (f32[32]{0:T(128)S(1)}, f32[32]{0:T(128)}, u32[]{:S(2)}) copy-start(f32[32]{0:T(128)} %get-tuple-element.72) | copy-start | bytes 388
  208.4 4.4 %copy-start.33 = (f32[32]{0:T(128)S(1)}, f32[32]{0:T(128)}, u32[]{:S(2)}) copy-start(f32[32]{0:T(128)} %get-tuple-element.73) | copy-start | bytes 388
  208.4 4.4 %copy-start.34 = (f32[32]{0:T(128)S(1)}, f32[32]{0:T(128)}, u32[]{:S(2)}) copy-start(f32[32]{0:T(128)} %get-tuple-element.74) | copy-start | bytes 388
  208.4 4.4 %copy-start.35 = (f32[32]{0:T(128)S(1)}, f32[32]{0:T(128)}, u32[]{:S(2)}) copy-start(f32[32]{0:T(128)} %get-tuple-element.75) | copy-start | bytes 388
  208.4 4.4 %copy-start.36 = (f32[32]{0:T(128)S(1)}, f32[32]{0:T(128)}, u32[]{:S(2)}) copy-start(f32[32]{0:T(128)} %get-tuple-element.76) | copy-start | bytes 388
  208.4 4.4 %copy-start.37 = (f32[32]{0:T(128)S(1)}, f32[32]{0:T(128)}, u32[]{:S(2)}) copy-start(f32[32]{0:T(128)} %get-tuple-element.81) | copy-start | bytes 388
  208.5 4.4 %copy-start.38 = (f32[32]{0:T(128)S(1)}, f32[32]{0:T(128)}, u32[]{:S(2)}) copy-start(f32[32]{0:T(128)} %get-tuple-element.82) | copy-start | bytes 388
  (10 other events, 28.0 us)
Sparse Core Ops, SparseCore 0:
  73.5 18.7 all-reduce.5
where the time goes:
time: 228 us; the launch traced here: 227 us
  blocking collectives  81.2 us (36%)
  other arithmetic  39.9 us (18%)
  local copies, waits for them, and re-layouts  35.5 us (16%)
  waiting for transfers between devices  34.4 us (15%)
  between operations  14.8 us (6%)
  starting transfers between devices  13.2 us (6%)
  matrix products  8.43 us (4%)
    psum x1, blocking collectives, shards(): totals = lax.psum((tile_part, wall_full, class_full), ('gx', 'gz', 'col'))  72.8 us
    psum x1, waiting for transfers between devices, shards(): scores = lax.psum(partial_scores, 'col')  18.9 us
    unnamed x105, local copies, waits for them, and re-layouts  11.5 us
    convert_element_type x1, other arithmetic, shards(): smoothed = smooth.astype(jnp.bfloat16)  11.2 us
    ppermute x4, waiting for transfers between devices, with_halo(): after = lax.ppermute(leading, axis, down)  9.77 us
    reduce_sum x3, other arithmetic, shards(): tile_terms.append(jnp.sum(shifted * grad_tile_vals, axis=(1, 2, 3)))  8.73 us
    ppermute x4, starting transfers between devices, with_halo(): before = lax.ppermute(last, axis, up)  8.43 us
    slice x3, local copies, waits for them, and re-layouts, with_halo(): leading = lax.slice_in_dim(value, 0, width, axis=dim)  6.44 us
  transfers between devices with their start and end apart: 9, of which 4 were waited for; matrix products, arithmetic and copies ran while one was open for 10% of the time, Pallas kernels for 0%

commit v1 on v0

v1 whole, which is shorter than its diff:
```python
import functools

import jax
import jax.numpy as jnp
from jax import lax
from jax.experimental import pallas as pl
from jax.experimental.pallas import tpu as pltpu
from jax.sharding import PartitionSpec as P

F32 = jnp.float32
BF16 = jnp.bfloat16
MESH = pl.DeviceIdType.MESH


def fold(value):
    total = value[0:8]
    for row in range(8, value.shape[0], 8):
        total = total + value[row : row + 8]
    return total


def rounded(value):
    return value.astype(BF16).astype(F32)


def kernel(
    dims,
    feat, labels, bands, tile_w, wall_w, class_w,
    out, small,
    recv, halo_out, halo_in, zfeat, smooth, stage, taps, band_rows, hid, slope,
    part_own, part_out, part_in, err, gwall, gsm, ghalo_out, ghalo_in, zgrad, gout, gstage,
    acc, red, sums,
    a_send, a_recv, own_sem, h_send, h_recv, s_send, s_recv, p_send, p_recv, e_send, e_recv,
    w_send, w_recv, g_send, g_recv, o_send, o_recv, r_send, r_recv,
):
    size, depth, cpg, chunks = dims
    per = cpg // chunks
    xs = 2 * size
    xgroups = xs // 8
    everyone = size * depth * 2
    gx, gz, col = lax.axis_index("gx"), lax.axis_index("gz"), lax.axis_index("col")
    me = (gx * depth + gz) * 2 + col
    other = 1 - col
    right, left = lax.rem(gz + 1, depth), lax.rem(gz + depth - 1, depth)
    chan0 = gx * cpg

    def peer(step):
        return lax.rem(gx + step, size)

    def source(step):
        return lax.rem(gx + size - step, size)

    def coords(step):
        index = lax.rem(me + step, everyone)
        return {
            "gx": index // (2 * depth),
            "gz": lax.rem(index // 2, depth),
            "col": lax.rem(index, 2),
        }

    barrier = pltpu.get_barrier_semaphore()

    @pl.loop(1, everyone)
    def _(step):
        pl.semaphore_signal(barrier, inc=1, device_id=coords(step), device_id_type=MESH)

    pl.semaphore_wait(barrier, everyone - 1)

    def remote(src, dst, send, rec, device):
        return pltpu.make_async_remote_copy(
            src_ref=src, dst_ref=dst, send_sem=send, recv_sem=rec,
            device_id=device, device_id_type=MESH,
        )

    def a_copy(chunk, step):
        return remote(
            feat.at[pl.ds(peer(step) * cpg + chunk * per, per)],
            recv.at[step, pl.ds(chunk * per, per)],
            a_send.at[chunk, step], a_recv.at[chunk, step], {"gx": peer(step)},
        )

    def h_copy(way, step):
        return remote(
            halo_out.at[peer(step)], halo_in.at[way, step],
            h_send.at[way, step], h_recv.at[way, step],
            {"gx": peer(step), "gz": right if way == 0 else left},
        )

    own_copy = pltpu.make_async_copy(feat.at[pl.ds(chan0, cpg)], recv.at[0], own_sem)
    own_copy.start()
    for step in range(1, size):
        a_copy(0, step).start()

    lane = lax.broadcasted_iota(jnp.int32, (8, 128), 1)
    quad = lane // 4

    @pl.loop(0, size)
    def _(group):
        for first in range(0, cpg, 4):
            packed = jnp.zeros((8, 128), F32)
            for c in range(first, min(first + 4, cpg)):
                stage[c] = feat[group * cpg + c].astype(F32)
                for xl in range(2):
                    rows = stage[c, pl.ds(xl, 32, stride=2), :]
                    for t in range(4):
                        m = (c - first) * 8 + xl * 4 + t
                        turned = pltpu.roll(rows[8 * t : 8 * t + 8], (2 + 4 * m) % 128, 1)
                        packed = jnp.where(quad == m, turned, packed)
            halo_out[group, pl.ds(first // 4 * 8, 8), :] = packed

    for way in range(2):
        for step in range(size):
            h_copy(way, step).start()
    for chunk in range(1, chunks):
        for step in range(1, size):
            a_copy(chunk, step).start()

    for k in range(9):
        band_rows[k] = jnp.broadcast_to(bands[pl.ds(32 * col, 48), k : k + 1], (48, 128))

    @pl.loop(0, cpg)
    def _(c):
        for k in range(9):
            taps[c, k] = wall_w[chan0 + c, k] * band_rows[k]
        for x_group in range(0, xs, 8):
            blank = jnp.zeros((8, 8, 128), F32)
            smooth[c, pl.ds(x_group, 8), pl.ds(pl.multiple_of(40 * col, 8), 8), :] = blank
            gwall[c, pl.ds(x_group, 8), pl.ds(pl.multiple_of(40 * col, 8), 8), :] = blank
        for q in range(40):
            acc[c, q] = jnp.zeros((8, 128), F32)

    red[...] = jnp.zeros((128, 128), F32)

    def shifts(value, edge):
        return (
            pltpu.roll(jnp.where(lane >= 126, edge, value), 2, 1),
            pltpu.roll(jnp.where(lane == 127, edge, value), 1, 1),
            value,
            pltpu.roll(jnp.where(lane == 0, edge, value), 127, 1),
            pltpu.roll(jnp.where(lane < 2, edge, value), 126, 1),
        )

    def filtered(field, c, x, flip):
        total = None
        for i in range(5):
            at = lax.rem(x + (4 - i if flip else i) - 2 + xs, xs)
            for j in range(5):
                term = tile_w[chan0 + c, 5 * i + j] * field[4 - j if flip else j, c, at]
                total = term if total is None else total + term
        return total

    def y_copy(ref, index, send, rec):
        src = pl.multiple_of(32 - 24 * col, 8)
        dst = pl.multiple_of(40 * col, 8)
        return remote(
            ref.at[index + (pl.ds(src, 8),)], ref.at[index + (pl.ds(dst, 8),)],
            send, rec, {"col": other},
        )

    def s_copy(c):
        return y_copy(smooth, (c, pl.ds(0, xs)), s_send.at[c], s_recv.at[c])

    own_copy.wait()
    for way in range(2):
        for step in range(size):
            h_copy(way, step).wait_recv()

    def edges_of(ref_left, ref_right):
        return jnp.where(lax.rem(lane, 4) < 2, ref_left, ref_right)

    for chunk in range(chunks):
        for step in range(1, size):
            a_copy(chunk, step).wait_recv()
        for c in range(chunk * per, chunk * per + per):

            @pl.loop(0, size)
            def _(step, c=c):
                s = source(step)
                stage[step] = recv[step, c].astype(F32)
                at = pl.ds(c // 4 * 8, 8)
                packed = edges_of(halo_in[0, step, at, :], halo_in[1, step, at, :])
                for xl in range(2):
                    rows = stage[step, pl.ds(xl, 32, stride=2), :]
                    for t in range(4):
                        m = c % 4 * 8 + xl * 4 + t
                        edge = pltpu.roll(packed, (126 - 4 * m) % 128, 1)
                        moved = shifts(rows[8 * t : 8 * t + 8], edge)
                        for j in range(5):
                            zfeat[j, c, 2 * s + xl, pl.ds(8 * t, 8), :] = moved[j]

            @pl.loop(0, xs)
            def _(x, c=c):
                smooth[c, x, pl.ds(8, 32), :] = rounded(filtered(zfeat, c, x, False))

            s_copy(c).start()

    for c in range(cpg):
        s_copy(c).wait_recv()

    def p_copy(step):
        return remote(
            part_out.at[step], part_in.at[step], p_send.at[step], p_recv.at[step],
            {"gx": peer(step)},
        )

    def scores_at(x):
        def body(c, totals):
            wall = None
            for k in range(9):
                term = taps[c, k, pl.ds(8, 32), :] * smooth[c, x, pl.ds(4 + k, 32), :]
                wall = term if wall is None else wall + term
            sig = jax.nn.sigmoid(wall)
            hidden = wall * sig
            hid[c, x] = hidden
            slope[c, x] = sig * (1.0 + wall * (1.0 - sig))
            return tuple(
                total + class_w[k, chan0 + c] * hidden for k, total in enumerate(totals)
            )

        return lax.fori_loop(0, cpg, body, tuple(jnp.zeros((32, 128), F32) for k in range(4)))

    @pl.loop(1, size)
    def _(step):
        for xl in range(2):
            totals = scores_at(2 * peer(step) + xl)
            for k in range(4):
                part_out[step, pl.ds((2 * k + xl) * 32, 32), :] = totals[k].astype(BF16)
        p_copy(step).start()

    for xl in range(2):
        totals = scores_at(2 * gx + xl)
        for k in range(4):
            part_own[pl.ds((2 * k + xl) * 32, 32), :] = totals[k]

    @pl.loop(1, size)
    def _(step):
        p_copy(step).wait_recv()
        part_own[...] = part_own[...] + part_in[step].astype(F32)

    for xl in range(2):
        marks = labels[pl.ds(64 * col + xl, 32, stride=2), :]
        for k in range(4):
            at = pl.ds((2 * k + xl) * 32, 32)
            err[0, at, :] = (part_own[at, :] - jnp.where(marks == k, 1.0, 0.0)).astype(BF16)

    def e_copy(step):
        return remote(
            err.at[0], err.at[step], e_send.at[step], e_recv.at[step], {"gx": peer(step)}
        )

    for step in range(1, size):
        e_copy(step).start()

    def w_copy(step):
        return y_copy(
            gwall, (pl.ds(0, cpg), pl.ds(2 * source(step), 2)), w_send.at[step], w_recv.at[step]
        )

    def wall_grads(step):
        for xl in range(2):
            x = 2 * source(step) + xl
            errors = [err[step, pl.ds((2 * k + xl) * 32, 32), :].astype(F32) for k in range(4)]

            @pl.loop(0, cpg)
            def _(c):
                hidden = hid[c, x]
                grad = None
                for k in range(4):
                    term = class_w[k, chan0 + c] * errors[k]
                    grad = term if grad is None else grad + term
                    acc[c, 34 + k] = acc[c, 34 + k] + fold(errors[k] * hidden)
                gwall[c, x, pl.ds(8, 32), :] = rounded(grad * slope[c, x])

        w_copy(step).start()

    wall_grads(0)

    @pl.loop(1, size)
    def _(step):
        e_copy(step).wait_recv()
        wall_grads(step)

    @pl.loop(0, size)
    def _(step):
        w_copy(step).wait_recv()

    def g_copy(way, c):
        return remote(
            ghalo_out.at[c], ghalo_in.at[way, c], g_send.at[way, c], g_recv.at[way, c],
            {"gz": right if way == 0 else left},
        )

    @pl.loop(0, cpg)
    def _(c):
        def body(x, sums9):
            grad = gwall[c, x, pl.ds(8, 32), :]
            total = None
            news = []
            for k in range(9):
                term = taps[c, k, pl.ds(12 - k, 32), :] * gwall[c, x, pl.ds(12 - k, 32), :]
                total = term if total is None else total + term
                product = grad * band_rows[k, pl.ds(8, 32), :] * smooth[c, x, pl.ds(4 + k, 32), :]
                news.append(sums9[k] + fold(product))
            gsm[c, x] = rounded(total)
            return tuple(news)

        sums9 = lax.fori_loop(0, xs, body, tuple(jnp.zeros((8, 128), F32) for k in range(9)))
        for k in range(9):
            acc[c, 25 + k] = sums9[k]

        @pl.loop(0, xgroups)
        def _(group):
            packed = jnp.zeros((8, 128), F32)
            for m in range(32):
                piece = gsm[c, group * 8 + m // 4, pl.ds(m % 4 * 8, 8), :]
                packed = jnp.where(quad == m, pltpu.roll(piece, (2 + 4 * m) % 128, 1), packed)
            ghalo_out[c, group] = packed

        for way in range(2):
            g_copy(way, c).start()

    def o_copy(chunk, step):
        return remote(
            gout.at[peer(step), pl.ds(chunk * per, per)],
            out.at[pl.ds(chan0 + chunk * per, per)],
            o_send.at[chunk, step], o_recv.at[chunk, step], {"gx": peer(step)},
        )

    @pl.loop(0, chunks)
    def _(chunk):
        @pl.loop(0, per)
        def _(lower):
            c = chunk * per + lower
            for way in range(2):
                g_copy(way, c).wait_recv()

            @pl.loop(0, xgroups)
            def _(group):
                packed = edges_of(ghalo_in[0, c, group], ghalo_in[1, c, group])
                for m in range(32):
                    at = pl.ds(m % 4 * 8, 8)
                    x = group * 8 + m // 4
                    edge = pltpu.roll(packed, (126 - 4 * m) % 128, 1)
                    moved = shifts(gsm[c, x, at, :], edge)
                    for j in range(5):
                        zgrad[j, c, x, at, :] = moved[j]

            @pl.loop(0, size)
            def _(s):
                for xl in range(2):
                    gstage[s, pl.ds(xl, 32, stride=2), :] = filtered(zgrad, c, 2 * s + xl, True)
                gout[s, c] = gstage[s].astype(BF16)

            out[chan0 + c] = gout[gx, c]

        for step in range(1, size):
            o_copy(chunk, step).start()

    row = lax.broadcasted_iota(jnp.int32, (8, 128), 0)

    @pl.loop(0, cpg)
    def _(c):
        def body(x, sums25):
            grad = gsm[c, x]
            news = []
            for i in range(5):
                at = lax.rem(x + i - 2 + xs, xs)
                for j in range(5):
                    news.append(sums25[5 * i + j] + fold(zfeat[j, c, at] * grad))
            return tuple(news)

        sums25 = lax.fori_loop(0, xs, body, tuple(jnp.zeros((8, 128), F32) for q in range(25)))
        for q in range(38):
            value = sums25[q] if q < 25 else acc[c, q]
            red[pl.ds(q, 1), :] = jnp.sum(value, axis=0, keepdims=True)
        line = lax.dot_general(
            jnp.ones((8, 128), F32), red[...], (((1,), (1,)), ((), ())),
            precision=lax.Precision.HIGHEST, preferred_element_type=F32,
        )
        before = jnp.where(c == 0, jnp.zeros((8, 128), F32), sums[me])
        sums[me] = jnp.where(row == c, line, before)

    def r_copy(step):
        return remote(sums.at[me], sums.at[me], r_send.at[step], r_recv.at[step], coords(step))

    @pl.loop(1, everyone)
    def _(step):
        r_copy(step).start()

    @pl.loop(1, everyone)
    def _(step):
        r_copy(step).wait_recv()

    @pl.loop(0, size)
    def _(group):
        total = sums[group * depth * 2]
        for member in range(1, depth * 2):
            total = total + sums[group * depth * 2 + member]
        small[group] = total

    for chunk in range(chunks):
        for step in range(1, size):
            o_copy(chunk, step).wait()
            a_copy(chunk, step).wait_send()
    for way in range(2):
        for step in range(size):
            h_copy(way, step).wait_send()
        for c in range(cpg):
            g_copy(way, c).wait_send()
    for c in range(cpg):
        s_copy(c).wait_send()
    for step in range(1, size):
        p_copy(step).wait_send()
        e_copy(step).wait_send()
    for step in range(size):
        w_copy(step).wait_send()

    @pl.loop(1, everyone)
    def _(step):
        r_copy(step).wait_send()


def shards(features, labels, grid_index, stretch, tile_filter, wall_filter, class_weight):
    chans, rows, cells_x, cells_z = features.shape
    size, depth = lax.axis_size("gx"), lax.axis_size("gz")
    volume = labels.shape[0] * cells_x * size * cells_z * depth
    cpg = chans // size
    chunks = min(4, cpg)
    per_dest = max(cpg // 4, 1) * 8
    xs = 2 * size
    everyone = size * depth * 2
    padded = jnp.pad(grid_index, (8, 8), constant_values=-1)
    onehot = (padded[:, None] == jnp.arange(stretch.shape[0], dtype=jnp.int32)).astype(F32)
    bands = jnp.dot(onehot, stretch, precision=lax.Precision.HIGHEST)
    dma = pltpu.SemaphoreType.DMA
    vmem = pl.BlockSpec(memory_space=pltpu.VMEM)
    smem = pl.BlockSpec(memory_space=pltpu.SMEM)
    grad, small = pl.pallas_call(
        functools.partial(kernel, (size, depth, cpg, chunks)),
        out_shape=(
            jax.ShapeDtypeStruct((chans, 64, 128), BF16),
            jax.ShapeDtypeStruct((size, 8, 128), F32),
        ),
        in_specs=[vmem, vmem, vmem, smem, smem, smem],
        out_specs=(vmem, vmem),
        scratch_shapes=[
            pltpu.VMEM((size, cpg, 64, 128), BF16),
            pltpu.VMEM((size, per_dest, 128), F32),
            pltpu.VMEM((2, size, per_dest, 128), F32),
            pltpu.VMEM((5, cpg, xs, 32, 128), F32),
            pltpu.VMEM((cpg, xs, 48, 128), F32),
            pltpu.VMEM((max(cpg, size), 64, 128), F32),
            pltpu.VMEM((cpg, 9, 48, 128), F32),
            pltpu.VMEM((9, 48, 128), F32),
            pltpu.VMEM((cpg, xs, 32, 128), F32),
            pltpu.VMEM((cpg, xs, 32, 128), F32),
            pltpu.VMEM((256, 128), F32),
            pltpu.VMEM((size, 256, 128), BF16),
            pltpu.VMEM((size, 256, 128), BF16),
            pltpu.VMEM((size, 256, 128), BF16),
            pltpu.VMEM((cpg, xs, 48, 128), F32),
            pltpu.VMEM((cpg, xs, 32, 128), F32),
            pltpu.VMEM((cpg, xs // 8, 8, 128), F32),
            pltpu.VMEM((2, cpg, xs // 8, 8, 128), F32),
            pltpu.VMEM((5, cpg, xs, 32, 128), F32),
            pltpu.VMEM((size, cpg, 64, 128), BF16),
            pltpu.VMEM((size, 64, 128), F32),
            pltpu.VMEM((cpg, 40, 8, 128), F32),
            pltpu.VMEM((128, 128), F32),
            pltpu.VMEM((everyone, 8, 128), F32),
            dma((chunks, size)), dma((chunks, size)), dma(()),
            dma((2, size)), dma((2, size)),
            dma((cpg,)), dma((cpg,)),
            dma((size,)), dma((size,)),
            dma((size,)), dma((size,)),
            dma((size,)), dma((size,)),
            dma((2, cpg)), dma((2, cpg)),
            dma((chunks, size)), dma((chunks, size)),
            dma((everyone,)), dma((everyone,)),
        ],
        compiler_params=pltpu.CompilerParams(
            collective_id=0, has_side_effects=True, vmem_limit_bytes=48 * 1024 * 1024
        ),
    )(
        features.reshape(chans, 64, 128), labels.reshape(128, 128), bands,
        tile_filter, wall_filter, class_weight,
    )
    table = small[:, :cpg].reshape(chans, 128) / volume
    return (
        grad.reshape(features.shape),
        table[:, :25],
        table[:, 25:34],
        table[:, 34:38].T,
    )


def solution(mesh):
    return jax.shard_map(
        shards,
        mesh=mesh,
        in_specs=(
            P(None, "col", ("group", "gx"), "gz"),
            P(None, ("group", "gx"), "gz"),
            P(),
            P(),
            P(),
            P(),
            P(),
        ),
        out_specs=(
            P(None, "col", ("group", "gx"), "gz"),
            P("group", None),
            P("group", None),
            P("group", None),
        ),
        check_vma=False,
    )
```

time: 228 us -> 70.5 us (0.31)
  blocking collectives: 81.2 us -> 0 us
  Pallas kernels: 0 us -> 63.9 us
  other arithmetic: 39.9 us -> 0.01 us
  waiting for transfers between devices: 34.4 us -> 0 us
  local copies, waits for them, and re-layouts: 35.5 us -> 5.36 us
  between operations: 14.8 us -> 0.69 us
  starting transfers between devices: 13.2 us -> 0 us
  matrix products: 8.43 us -> 0.21 us
    psum x1 -> x0, blocking collectives: 72.8 us -> none  [shards(): totals = lax.psum((tile_part, wall_full, class_full), ('gx', 'gz', 'col'))]
    pallas_call x0 -> x1, Pallas kernels: none -> 63.9 us  [shards(): pl.pallas_call(functools.partial(kernel, (size, depth, cpg, chunks)), out...]
    convert_element_type x3 -> x0, other arithmetic: 19.4 us -> none  [the longest x1 11.2 us: shards(): smoothed = smooth.astype(jnp.bfloat16)]
    psum x1 -> x0, waiting for transfers between devices: 18.9 us -> none  [shards(): scores = lax.psum(partial_scores, 'col')]
    ppermute x8 -> x0, waiting for transfers between devices: 15.5 us -> none  [the longest x4 9.77 us: with_halo(): after = lax.ppermute(leading, axis, down)]
    slice x7 -> x2, local copies, waits for them, and re-layouts: 14 us -> 0.14 us  [the longest x1 0.07 us: shards(): table[:, 25:34]]
    ppermute x8 -> x0, starting transfers between devices: 13.2 us -> none  [the longest x4 8.43 us: with_halo(): before = lax.ppermute(last, axis, up)]
    ppermute x4 -> x0, local copies, waits for them, and re-layouts: 8.78 us -> none  [the longest x2 4.41 us: with_halo(): before = lax.ppermute(last, axis, up)]
  transfers between devices with their start and end apart: 9 -> 0, of which waited for: 4 -> 0; matrix products, arithmetic and copies ran while one was open for 10% -> 0% of each run, Pallas kernels for 0% -> 0%
where the time goes in v1:
time: 70.5 us; the launch traced here: 70.2 us
  Pallas kernels  63.9 us (91%)
  local copies, waits for them, and re-layouts  5.36 us (8%)
    pallas_call x1, Pallas kernels, shards(): pl.pallas_call(functools.partial(kernel, (size, depth, cpg, chunks)), out...  63.9 us
    unnamed x16, local copies, waits for them, and re-layouts  4.46 us

profile of v1, /device:TPU:0, one launch (start us, length us, event | category | flops | bytes accessed | tf_op | source)
XLA Modules:
  0.0 70.2 jit_solution(8798141312711826402)
XLA Ops:
  0.6 0.0 copy-start
  0.6 0.0 copy-start.2
  0.7 0.8 %pad.4 = s32[80]{0:T(128)S(1)} pad(s32[64]{0:T(128)} %param.9, s32[]{:T(128)} %constant.1.clone.1), padding=8_8 | pad | bytes 580 | tf_op jit(solution)/shard_map/jit(_pad)/pad | solution.py:432
  1.4 0.8 %copy.12.wall_w = f32[32,9]{1,0:T(8,128)S(1)} copy(f32[32,9]{0,1:T(8,128)} %param.12) | data formatting | bytes 2304 | tf_op args[5]
  2.2 0.0 copy-done
  2.2 0.0 copy-start.3
  2.2 0.0 copy-start.4
  2.2 0.2 fusion.bands
  2.4 0.0 copy-done.2
  2.4 0.5 copy-done.3
  2.9 0.0 copy-done.4
  2.9 0.0 copy-start.1
  2.9 1.0 %copy-done.1 = bf16[32,32,2,128]{3,2,1,0:T(2,128)(2,1)S(1)} copy-done((bf16[32,32,2,128]{3,2,1,0:T(2,128)(2,1)S(1)}, bf16[32,32,2,128]{3,2,1,0:T(2,128)(2,1)}, u32[]{:S(2)}) %copy-start.1) | copy-done | bytes 524312
  4.0 63.9 %shard_map.102 = (bf16[32,64,128]{2,1,0:T(8,128)(2,1)S(1)}, f32[4,8,128]{2,1,0:T(8,128)S(1)}) custom-call(bf16[32,64,128]{2,1,0:T(8,128)(2,1)S(1)} %bitcast.8, s32[128,128]{1,0:T(8,128)S(1)} %bitcast.10, f32[80,9]{1,0:T(8,128)S(1)} %fusion.bands, f32[32,25]{1,0:T(8,128)S(1)} %copy-done.3, f32[32,9]{1,0:T(8,128)S(1)} %copy.12.wall_w, f32[4,32]{1,0:T(4,128)S(1)} %copy-done.4), custom_call_target="tpu_custom_call" | custom-call | tf_op jit(solution)/shard_map/pallas_call | solution.py:438
  67.9 0.0 copy-start.5
  67.9 0.1 slice.13
  68.0 0.7 copy.16
  68.6 0.0 copy-done.5
  68.6 0.1 slice.14
  68.7 0.7 copy.17
  69.4 0.8 %copy.19 = bf16[32,32,2,128]{3,2,1,0:T(2,128)(2,1)} copy(bf16[32,32,2,128]{3,2,1,0:T(2,128)(2,1)S(1)} %bitcast.9) | data formatting | bytes 1048576
  (1 shorter events, 0.0 us)
Async XLA Ops:
  0.6 1.6 %copy-start = (f32[16,9]{1,0:T(8,128)S(1)}, f32[16,9]{1,0:T(8,128)}, u32[]{:S(2)}) copy-start(f32[16,9]{1,0:T(8,128)} %param.10) | copy-start | bytes 1732
  0.6 1.8 %copy-start.2 = (s32[64,2,128]{2,1,0:T(2,128)S(1)}, s32[64,2,128]{2,1,0:T(2,128)}, u32[]{:S(2)}) copy-start(s32[64,2,128]{2,1,0:T(2,128)} %param.8) | copy-start | bytes 196612
  2.2 0.7 %copy-start.3 = (f32[32,25]{1,0:T(8,128)S(1)}, f32[32,25]{1,0:T(8,128)}, u32[]{:S(2)}) copy-start(f32[32,25]{1,0:T(8,128)} %tile_w.1) | copy-start | bytes 9604
  2.2 0.7 %copy-start.4 = (f32[4,32]{1,0:T(4,128)S(1)}, f32[4,32]{1,0:T(4,128)}, u32[]{:S(2)}) copy-start(f32[4,32]{1,0:T(4,128)} %class_w.1) | copy-start | bytes 1540
  2.9 1.0 %copy-start.1 = (bf16[32,32,2,128]{3,2,1,0:T(2,128)(2,1)S(1)}, bf16[32,32,2,128]{3,2,1,0:T(2,128)(2,1)}, u32[]{:S(2)}) copy-start(bf16[32,32,2,128]{3,2,1,0:T(2,128)(2,1)} %param.7) | copy-start | bytes 1572868
  67.9 0.8 %copy-start.5 = (f32[32,128]{1,0:T(8,128)}, f32[32,128]{1,0:T(8,128)S(1)}, u32[]{:S(2)}) copy-start(f32[32,128]{1,0:T(8,128)S(1)} %multiply_bitcast_fusion) | copy-start | bytes 49156

commit v2 on v1

--- a/solution.py
+++ b/solution.py
@@ -26,14 +26,14 @@
 def kernel(
     dims,
     feat, labels, bands, tile_w, wall_w, class_w,
-    out, small,
-    recv, halo_out, halo_in, zfeat, smooth, stage, taps, band_rows, hid, slope,
+    out, tile_out, wall_out, class_out,
+    recv, band_pad, halo_out, halo_in, zfeat, smooth, stage, taps, band_rows, hid, slope,
     part_own, part_out, part_in, err, gwall, gsm, ghalo_out, ghalo_in, zgrad, gout, gstage,
     acc, red, sums,
     a_send, a_recv, own_sem, h_send, h_recv, s_send, s_recv, p_send, p_recv, e_send, e_recv,
     w_send, w_recv, g_send, g_recv, o_send, o_recv, r_send, r_recv,
 ):
-    size, depth, cpg, chunks = dims
+    size, depth, cpg, chunks, volume = dims
     per = cpg // chunks
     xs = 2 * size
     xgroups = xs // 8
@@ -115,13 +115,16 @@
         for step in range(1, size):
             a_copy(chunk, step).start()
 
+    band_pad[0:8] = jnp.zeros((8, 9), F32)
+    band_pad[8:72] = bands[...]
+    band_pad[72:80] = jnp.zeros((8, 9), F32)
     for k in range(9):
-        band_rows[k] = jnp.broadcast_to(bands[pl.ds(32 * col, 48), k : k + 1], (48, 128))
+        band_rows[k] = jnp.broadcast_to(band_pad[pl.ds(32 * col, 48), k : k + 1], (48, 128))
 
     @pl.loop(0, cpg)
     def _(c):
         for k in range(9):
-            taps[c, k] = wall_w[chan0 + c, k] * band_rows[k]
+            taps[c, k] = wall_w[k, chan0 + c] * band_rows[k]
         for x_group in range(0, xs, 8):
             blank = jnp.zeros((8, 8, 128), F32)
             smooth[c, pl.ds(x_group, 8), pl.ds(pl.multiple_of(40 * col, 8), 8), :] = blank
@@ -173,7 +176,7 @@
             a_copy(chunk, step).wait_recv()
         for c in range(chunk * per, chunk * per + per):
 
-            @pl.loop(0, size)
+            @pl.loop(0, size, unroll=2)
             def _(step, c=c):
                 s = source(step)
                 stage[step] = recv[step, c].astype(F32)
@@ -188,7 +191,7 @@
                         for j in range(5):
                             zfeat[j, c, 2 * s + xl, pl.ds(8 * t, 8), :] = moved[j]
 
-            @pl.loop(0, xs)
+            @pl.loop(0, xs, unroll=4)
             def _(x, c=c):
                 smooth[c, x, pl.ds(8, 32), :] = rounded(filtered(zfeat, c, x, False))
 
@@ -217,7 +220,9 @@
                 total + class_w[k, chan0 + c] * hidden for k, total in enumerate(totals)
             )
 
-        return lax.fori_loop(0, cpg, body, tuple(jnp.zeros((32, 128), F32) for k in range(4)))
+        return lax.fori_loop(
+            0, cpg, body, tuple(jnp.zeros((32, 128), F32) for k in range(4)), unroll=min(4, cpg)
+        )
 
     @pl.loop(1, size)
     def _(step):
@@ -261,7 +266,7 @@
             x = 2 * source(step) + xl
             errors = [err[step, pl.ds((2 * k + xl) * 32, 32), :].astype(F32) for k in range(4)]
 
-            @pl.loop(0, cpg)
+            @pl.loop(0, cpg, unroll=min(4, cpg))
             def _(c):
                 hidden = hid[c, x]
                 grad = None
@@ -304,7 +309,7 @@
             gsm[c, x] = rounded(total)
             return tuple(news)
 
-        sums9 = lax.fori_loop(0, xs, body, tuple(jnp.zeros((8, 128), F32) for k in range(9)))
+        sums9 = lax.fori_loop(0, xs, body, tuple(jnp.zeros((8, 128), F32) for k in range(9)), unroll=2)
         for k in range(9):
             acc[c, 25 + k] = sums9[k]
 
@@ -345,7 +350,7 @@
                     for j in range(5):
                         zgrad[j, c, x, at, :] = moved[j]
 
-            @pl.loop(0, size)
+            @pl.loop(0, size, unroll=2)
             def _(s):
                 for xl in range(2):
                     gstage[s, pl.ds(xl, 32, stride=2), :] = filtered(zgrad, c, 2 * s + xl, True)
@@ -369,7 +374,7 @@
                     news.append(sums25[5 * i + j] + fold(zfeat[j, c, at] * grad))
             return tuple(news)
 
-        sums25 = lax.fori_loop(0, xs, body, tuple(jnp.zeros((8, 128), F32) for q in range(25)))
+        sums25 = lax.fori_loop(0, xs, body, tuple(jnp.zeros((8, 128), F32) for q in range(25)), unroll=2)
         for q in range(38):
             value = sums25[q] if q < 25 else acc[c, q]
             red[pl.ds(q, 1), :] = jnp.sum(value, axis=0, keepdims=True)
@@ -396,7 +401,13 @@
         total = sums[group * depth * 2]
         for member in range(1, depth * 2):
             total = total + sums[group * depth * 2 + member]
-        small[group] = total
+        red[pl.ds(group * cpg, cpg), :] = total[0:cpg] / volume
+
+    turned = red[...].T
+    chans = size * cpg
+    tile_out[...] = red[0:chans, 0:25]
+    wall_out[...] = turned[25:34, 0:chans]
+    class_out[...] = turned[34:38, 0:chans]
 
     for chunk in range(chunks):
         for step in range(1, size):
@@ -429,22 +440,24 @@
     per_dest = max(cpg // 4, 1) * 8
     xs = 2 * size
     everyone = size * depth * 2
-    padded = jnp.pad(grid_index, (8, 8), constant_values=-1)
-    onehot = (padded[:, None] == jnp.arange(stretch.shape[0], dtype=jnp.int32)).astype(F32)
+    onehot = (grid_index[:, None] == jnp.arange(stretch.shape[0], dtype=jnp.int32)).astype(F32)
     bands = jnp.dot(onehot, stretch, precision=lax.Precision.HIGHEST)
     dma = pltpu.SemaphoreType.DMA
     vmem = pl.BlockSpec(memory_space=pltpu.VMEM)
     smem = pl.BlockSpec(memory_space=pltpu.SMEM)
-    grad, small = pl.pallas_call(
-        functools.partial(kernel, (size, depth, cpg, chunks)),
+    grad, tile_grad, wall_grad, class_grad = pl.pallas_call(
+        functools.partial(kernel, (size, depth, cpg, chunks, volume)),
         out_shape=(
             jax.ShapeDtypeStruct((chans, 64, 128), BF16),
-            jax.ShapeDtypeStruct((size, 8, 128), F32),
+            jax.ShapeDtypeStruct((chans, 25), F32),
+            jax.ShapeDtypeStruct((9, chans), F32),
+            jax.ShapeDtypeStruct((4, chans), F32),
         ),
         in_specs=[vmem, vmem, vmem, smem, smem, smem],
-        out_specs=(vmem, vmem),
+        out_specs=(vmem, vmem, vmem, vmem),
         scratch_shapes=[
             pltpu.VMEM((size, cpg, 64, 128), BF16),
+            pltpu.VMEM((80, 9), F32),
             pltpu.VMEM((size, per_dest, 128), F32),
             pltpu.VMEM((2, size, per_dest, 128), F32),
             pltpu.VMEM((5, cpg, xs, 32, 128), F32),
@@ -483,15 +496,9 @@
         ),
     )(
         features.reshape(chans, 64, 128), labels.reshape(128, 128), bands,
-        tile_filter, wall_filter, class_weight,
+        tile_filter, wall_filter.T, class_weight,
     )
-    table = small[:, :cpg].reshape(chans, 128) / volume
-    return (
-        grad.reshape(features.shape),
-        table[:, :25],
-        table[:, 25:34],
-        table[:, 34:38].T,
-    )
+    return grad.reshape(features.shape), tile_grad, wall_grad.T, class_grad
 
 
 def solution(mesh):

time: 70.5 us -> 68.8 us (0.976)
  Pallas kernels: 63.9 us -> 61.2 us
    pallas_call x1, Pallas kernels: 63.9 us -> 61.2 us  [shards(): pl.pallas_call(functools.partial(kernel, (size, depth, cpg, chunks, volum...]
    unnamed x16, local copies, waits for them, and re-layouts: 4.46 us -> 5.72 us
    pad x1 -> x0, local copies, waits for them, and re-layouts: 0.76 us -> none  [shards(): padded = jnp.pad(grid_index, (8, 8), constant_values=-1)]
where the time goes in v2:
time: 68.8 us; the launch traced here: 68.4 us
  Pallas kernels  61.2 us (89%)
  local copies, waits for them, and re-layouts  5.72 us (8%)
  matrix products  0.87 us (1%)
  between operations  0.69 us (1%)
    pallas_call x1, Pallas kernels, shards(): pl.pallas_call(functools.partial(kernel, (size, depth, cpg, chunks, volum...  61.2 us
    unnamed x16, local copies, waits for them, and re-layouts  5.72 us

profile of v2, /device:TPU:0, one launch (start us, length us, event | category | flops | bytes accessed | tf_op | source)
XLA Modules:
  0.0 68.4 jit_solution(2412130585921756764)
XLA Ops:
  0.6 0.0 copy-start
  0.6 0.0 copy-start.2
  0.7 0.7 copy-done
  1.3 0.0 copy-start.5
  1.3 0.9 %fusion.bands = f32[64,9]{1,0:T(8,128)S(1)} fusion(f32[16,9]{1,0:T(8,128)S(1)} %copy-done, s32[64]{0:T(128)} %param.9), kind=kOutput, calls=%fused_computation.1 | convolution fusion | flops 111616 | bytes 3136 | tf_op jit(solution)/shard_map/dot_general | solution.py:444
  2.2 0.0 copy-done.2
  2.2 0.0 copy-done.5
  2.2 0.0 copy-start.1
  2.2 1.0 %copy-done.1 = bf16[32,32,2,128]{3,2,1,0:T(2,128)(2,1)S(1)} copy-done((bf16[32,32,2,128]{3,2,1,0:T(2,128)(2,1)S(1)}, bf16[32,32,2,128]{3,2,1,0:T(2,128)(2,1)}, u32[]{:S(2)}) %copy-start.1) | copy-done | bytes 524312
  3.3 0.0 copy-start.3
  3.3 0.7 %copy-done.3 = f32[32,25]{1,0:T(8,128)S(1)} copy-done((f32[32,25]{1,0:T(8,128)S(1)}, f32[32,25]{1,0:T(8,128)}, u32[]{:S(2)}) %copy-start.3) | copy-done | bytes 3224
  4.0 0.0 copy-start.4
  4.0 0.7 %copy-done.4 = f32[32,9]{0,1:T(8,128)S(1)} copy-done((f32[32,9]{0,1:T(8,128)S(1)}, f32[32,9]{0,1:T(8,128)}, u32[]{:S(2)}) %copy-start.4) | copy-done | bytes 1176
  4.7 61.2 %shard_map.102 = (bf16[32,64,128]{2,1,0:T(8,128)(2,1)S(1)}, f32[32,25]{1,0:T(8,128)S(1)}, f32[9,32]{1,0:T(8,128)S(1)}, f32[4,32]{1,0:T(4,128)S(1)}) custom-call(bf16[32,64,128]{2,1,0:T(8,128)(2,1)S(1)} %bitcast.6, s32[128,128]{1,0:T(8,128)S(1)} %bitcast.8, f32[64,9]{1,0:T(8,128)S(1)} %fusion.bands, f32[32,25]{1,0:T(8,128)S(1)} %copy-done.3, ...), custom_call_target="tpu_custom_call" | custom-call | tf_op jit(solution)/shard_map/pallas_call | solution.py:448
  65.9 0.8 %copy.17 = bf16[32,32,2,128]{3,2,1,0:T(2,128)(2,1)} copy(bf16[32,32,2,128]{3,2,1,0:T(2,128)(2,1)S(1)} %bitcast.7) | data formatting | bytes 1048576
  66.7 0.6 copy.18
  67.3 0.6 copy.19
  67.9 0.6 copy.20
Async XLA Ops:
  0.6 0.7 %copy-start = (f32[16,9]{1,0:T(8,128)S(1)}, f32[16,9]{1,0:T(8,128)}, u32[]{:S(2)}) copy-start(f32[16,9]{1,0:T(8,128)} %param.10) | copy-start | bytes 1732
  0.6 1.6 %copy-start.2 = (s32[64,2,128]{2,1,0:T(2,128)S(1)}, s32[64,2,128]{2,1,0:T(2,128)}, u32[]{:S(2)}) copy-start(s32[64,2,128]{2,1,0:T(2,128)} %param.8) | copy-start | bytes 196612
  1.3 0.9 %copy-start.5 = (f32[4,32]{1,0:T(4,128)S(1)}, f32[4,32]{1,0:T(4,128)}, u32[]{:S(2)}) copy-start(f32[4,32]{1,0:T(4,128)} %class_w.1) | copy-start | bytes 1540
  2.2 1.0 %copy-start.1 = (bf16[32,32,2,128]{3,2,1,0:T(2,128)(2,1)S(1)}, bf16[32,32,2,128]{3,2,1,0:T(2,128)(2,1)}, u32[]{:S(2)}) copy-start(bf16[32,32,2,128]{3,2,1,0:T(2,128)(2,1)} %param.7) | copy-start | bytes 1572868
  3.3 0.7 %copy-start.3 = (f32[32,25]{1,0:T(8,128)S(1)}, f32[32,25]{1,0:T(8,128)}, u32[]{:S(2)}) copy-start(f32[32,25]{1,0:T(8,128)} %tile_w.1) | copy-start | bytes 9604
  4.0 0.7 %copy-start.4 = (f32[32,9]{0,1:T(8,128)S(1)}, f32[32,9]{0,1:T(8,128)}, u32[]{:S(2)}) copy-start(f32[32,9]{0,1:T(8,128)} %param.12) | copy-start | bytes 3460

commit v3 on v2

--- a/solution.py
+++ b/solution.py
@@ -29,7 +29,7 @@
     out, tile_out, wall_out, class_out,
     recv, band_pad, halo_out, halo_in, zfeat, smooth, stage, taps, band_rows, hid, slope,
     part_own, part_out, part_in, err, gwall, gsm, ghalo_out, ghalo_in, zgrad, gout, gstage,
-    acc, red, sums,
+    taps_back, red, sums,
     a_send, a_recv, own_sem, h_send, h_recv, s_send, s_recv, p_send, p_recv, e_send, e_recv,
     w_send, w_recv, g_send, g_recv, o_send, o_recv, r_send, r_recv,
 ):
@@ -129,8 +129,8 @@
             blank = jnp.zeros((8, 8, 128), F32)
             smooth[c, pl.ds(x_group, 8), pl.ds(pl.multiple_of(40 * col, 8), 8), :] = blank
             gwall[c, pl.ds(x_group, 8), pl.ds(pl.multiple_of(40 * col, 8), 8), :] = blank
-        for q in range(40):
-            acc[c, q] = jnp.zeros((8, 128), F32)
+        for k in range(9):
+            taps_back[c, k] = taps[c, k, pl.ds(12 - k, 32), :]
 
     red[...] = jnp.zeros((128, 128), F32)
 
@@ -261,19 +261,20 @@
             gwall, (pl.ds(0, cpg), pl.ds(2 * source(step), 2)), w_send.at[step], w_recv.at[step]
         )
 
+    def errors_at(step, xl):
+        return [err[step, pl.ds((2 * k + xl) * 32, 32), :].astype(F32) for k in range(4)]
+
     def wall_grads(step):
         for xl in range(2):
             x = 2 * source(step) + xl
-            errors = [err[step, pl.ds((2 * k + xl) * 32, 32), :].astype(F32) for k in range(4)]
+            errors = errors_at(step, xl)
 
             @pl.loop(0, cpg, unroll=min(4, cpg))
             def _(c):
-                hidden = hid[c, x]
                 grad = None
                 for k in range(4):
                     term = class_w[k, chan0 + c] * errors[k]
                     grad = term if grad is None else grad + term
-                    acc[c, 34 + k] = acc[c, 34 + k] + fold(errors[k] * hidden)
                 gwall[c, x, pl.ds(8, 32), :] = rounded(grad * slope[c, x])
 
         w_copy(step).start()
@@ -297,21 +298,13 @@
 
     @pl.loop(0, cpg)
     def _(c):
-        def body(x, sums9):
-            grad = gwall[c, x, pl.ds(8, 32), :]
+        @pl.loop(0, xs, unroll=2)
+        def _(x):
             total = None
-            news = []
             for k in range(9):
-                term = taps[c, k, pl.ds(12 - k, 32), :] * gwall[c, x, pl.ds(12 - k, 32), :]
+                term = taps_back[c, k] * gwall[c, x, pl.ds(12 - k, 32), :]
                 total = term if total is None else total + term
-                product = grad * band_rows[k, pl.ds(8, 32), :] * smooth[c, x, pl.ds(4 + k, 32), :]
-                news.append(sums9[k] + fold(product))
             gsm[c, x] = rounded(total)
-            return tuple(news)
-
-        sums9 = lax.fori_loop(0, xs, body, tuple(jnp.zeros((8, 128), F32) for k in range(9)), unroll=2)
-        for k in range(9):
-            acc[c, 25 + k] = sums9[k]
 
         @pl.loop(0, xgroups)
         def _(group):
@@ -375,8 +368,31 @@
             return tuple(news)
 
         sums25 = lax.fori_loop(0, xs, body, tuple(jnp.zeros((8, 128), F32) for q in range(25)), unroll=2)
-        for q in range(38):
-            value = sums25[q] if q < 25 else acc[c, q]
+
+        def wall_body(x, sums9):
+            grad = gwall[c, x, pl.ds(8, 32), :]
+            news = []
+            for k in range(9):
+                product = grad * band_rows[k, pl.ds(8, 32), :] * smooth[c, x, pl.ds(4 + k, 32), :]
+                news.append(sums9[k] + fold(product))
+            return tuple(news)
+
+        def class_body(step, sums4):
+            news = list(sums4)
+            for xl in range(2):
+                hidden = hid[c, 2 * source(step) + xl]
+                errors = errors_at(step, xl)
+                for k in range(4):
+                    news[k] = news[k] + fold(errors[k] * hidden)
+            return tuple(news)
+
+        sums9 = lax.fori_loop(
+            0, xs, wall_body, tuple(jnp.zeros((8, 128), F32) for k in range(9)), unroll=2
+        )
+        sums4 = lax.fori_loop(
+            0, size, class_body, tuple(jnp.zeros((8, 128), F32) for k in range(4)), unroll=2
+        )
+        for q, value in enumerate(sums25 + sums9 + sums4):
             red[pl.ds(q, 1), :] = jnp.sum(value, axis=0, keepdims=True)
         line = lax.dot_general(
             jnp.ones((8, 128), F32), red[...], (((1,), (1,)), ((), ())),
@@ -478,7 +494,7 @@
             pltpu.VMEM((5, cpg, xs, 32, 128), F32),
             pltpu.VMEM((size, cpg, 64, 128), BF16),
             pltpu.VMEM((size, 64, 128), F32),
-            pltpu.VMEM((cpg, 40, 8, 128), F32),
+            pltpu.VMEM((cpg, 9, 32, 128), F32),
             pltpu.VMEM((128, 128), F32),
             pltpu.VMEM((everyone, 8, 128), F32),
             dma((chunks, size)), dma((chunks, size)), dma(()),

time: 68.8 us -> 70.5 us (1.025)
  Pallas kernels: 61.2 us -> 62.8 us
    pallas_call x1, Pallas kernels: 61.2 us -> 62.8 us  [shards(): pl.pallas_call(functools.partial(kernel, (size, depth, cpg, chunks, volum...]
where the time goes in v3:
time: 70.5 us; the launch traced here: 70.1 us
  Pallas kernels  62.8 us (89%)
  local copies, waits for them, and re-layouts  5.72 us (8%)
  matrix products  0.87 us (1%)
    pallas_call x1, Pallas kernels, shards(): pl.pallas_call(functools.partial(kernel, (size, depth, cpg, chunks, volum...  62.8 us
    unnamed x16, local copies, waits for them, and re-layouts  5.72 us

profile of v3, /device:TPU:0, one launch (start us, length us, event | category | flops | bytes accessed | tf_op | source)
XLA Modules:
  0.0 70.1 jit_solution(9575763020515230099)
XLA Ops:
  0.6 0.0 copy-start
  0.6 0.0 copy-start.2
  0.7 0.7 copy-done
  1.3 0.0 copy-start.5
  1.3 0.9 %fusion.bands = f32[64,9]{1,0:T(8,128)S(1)} fusion(f32[16,9]{1,0:T(8,128)S(1)} %copy-done, s32[64]{0:T(128)} %param.9), kind=kOutput, calls=%fused_computation.1 | convolution fusion | flops 111616 | bytes 3136 | tf_op jit(solution)/shard_map/dot_general | solution.py:460
  2.2 0.0 copy-done.2
  2.2 0.0 copy-done.5
  2.2 0.0 copy-start.1
  2.2 1.0 %copy-done.1 = bf16[32,32,2,128]{3,2,1,0:T(2,128)(2,1)S(1)} copy-done((bf16[32,32,2,128]{3,2,1,0:T(2,128)(2,1)S(1)}, bf16[32,32,2,128]{3,2,1,0:T(2,128)(2,1)}, u32[]{:S(2)}) %copy-start.1) | copy-done | bytes 524312
  3.3 0.0 copy-start.3
  3.3 0.7 %copy-done.3 = f32[32,25]{1,0:T(8,128)S(1)} copy-done((f32[32,25]{1,0:T(8,128)S(1)}, f32[32,25]{1,0:T(8,128)}, u32[]{:S(2)}) %copy-start.3) | copy-done | bytes 3224
  4.0 0.0 copy-start.4
  4.0 0.7 copy-done.4
  4.7 62.8 %shard_map.102 = (bf16[32,64,128]{2,1,0:T(8,128)(2,1)S(1)}, f32[32,25]{1,0:T(8,128)S(1)}, f32[9,32]{1,0:T(8,128)S(1)}, f32[4,32]{1,0:T(4,128)S(1)}) custom-call(bf16[32,64,128]{2,1,0:T(8,128)(2,1)S(1)} %bitcast.6, s32[128,128]{1,0:T(8,128)S(1)} %bitcast.8, f32[64,9]{1,0:T(8,128)S(1)} %fusion.bands, f32[32,25]{1,0:T(8,128)S(1)} %copy-done.3, ...), custom_call_target="tpu_custom_call" | custom-call | tf_op jit(solution)/shard_map/pallas_call | solution.py:464
  67.5 0.8 %copy.17 = bf16[32,32,2,128]{3,2,1,0:T(2,128)(2,1)} copy(bf16[32,32,2,128]{3,2,1,0:T(2,128)(2,1)S(1)} %bitcast.7) | data formatting | bytes 1048576
  68.3 0.6 copy.18
  69.0 0.6 copy.19
  69.5 0.6 copy.20
Async XLA Ops:
  0.6 0.7 %copy-start = (f32[16,9]{1,0:T(8,128)S(1)}, f32[16,9]{1,0:T(8,128)}, u32[]{:S(2)}) copy-start(f32[16,9]{1,0:T(8,128)} %param.10) | copy-start | bytes 1732
  0.6 1.6 %copy-start.2 = (s32[64,2,128]{2,1,0:T(2,128)S(1)}, s32[64,2,128]{2,1,0:T(2,128)}, u32[]{:S(2)}) copy-start(s32[64,2,128]{2,1,0:T(2,128)} %param.8) | copy-start | bytes 196612
  1.3 0.9 %copy-start.5 = (f32[4,32]{1,0:T(4,128)S(1)}, f32[4,32]{1,0:T(4,128)}, u32[]{:S(2)}) copy-start(f32[4,32]{1,0:T(4,128)} %class_w.1) | copy-start | bytes 1540
  2.2 1.0 %copy-start.1 = (bf16[32,32,2,128]{3,2,1,0:T(2,128)(2,1)S(1)}, bf16[32,32,2,128]{3,2,1,0:T(2,128)(2,1)}, u32[]{:S(2)}) copy-start(bf16[32,32,2,128]{3,2,1,0:T(2,128)(2,1)} %param.7) | copy-start | bytes 1572868
  3.3 0.7 %copy-start.3 = (f32[32,25]{1,0:T(8,128)S(1)}, f32[32,25]{1,0:T(8,128)}, u32[]{:S(2)}) copy-start(f32[32,25]{1,0:T(8,128)} %tile_w.1) | copy-start | bytes 9604
  4.0 0.7 copy-start.4

commit v4 on v3

--- a/solution.py
+++ b/solution.py
@@ -29,7 +29,7 @@
     out, tile_out, wall_out, class_out,
     recv, band_pad, halo_out, halo_in, zfeat, smooth, stage, taps, band_rows, hid, slope,
     part_own, part_out, part_in, err, gwall, gsm, ghalo_out, ghalo_in, zgrad, gout, gstage,
-    taps_back, red, sums,
+    taps_back, acc, red, sums,
     a_send, a_recv, own_sem, h_send, h_recv, s_send, s_recv, p_send, p_recv, e_send, e_recv,
     w_send, w_recv, g_send, g_recv, o_send, o_recv, r_send, r_recv,
 ):
@@ -286,6 +286,34 @@
         e_copy(step).wait_recv()
         wall_grads(step)
 
+    @pl.loop(0, cpg)
+    def _(c):
+        def wall_body(x, sums9):
+            grad = gwall[c, x, pl.ds(8, 32), :]
+            news = []
+            for k in range(9):
+                product = grad * band_rows[k, pl.ds(8, 32), :] * smooth[c, x, pl.ds(4 + k, 32), :]
+                news.append(sums9[k] + fold(product))
+            return tuple(news)
+
+        def class_body(step, sums4):
+            news = list(sums4)
+            for xl in range(2):
+                hidden = hid[c, 2 * source(step) + xl]
+                errors = errors_at(step, xl)
+                for k in range(4):
+                    news[k] = news[k] + fold(errors[k] * hidden)
+            return tuple(news)
+
+        sums9 = lax.fori_loop(
+            0, xs, wall_body, tuple(jnp.zeros((8, 128), F32) for k in range(9)), unroll=2
+        )
+        sums4 = lax.fori_loop(
+            0, size, class_body, tuple(jnp.zeros((8, 128), F32) for k in range(4)), unroll=2
+        )
+        for q, value in enumerate(sums9 + sums4):
+            acc[c, q] = value
+
     @pl.loop(0, size)
     def _(step):
         w_copy(step).wait_recv()
@@ -368,31 +396,8 @@
             return tuple(news)
 
         sums25 = lax.fori_loop(0, xs, body, tuple(jnp.zeros((8, 128), F32) for q in range(25)), unroll=2)
-
-        def wall_body(x, sums9):
-            grad = gwall[c, x, pl.ds(8, 32), :]
-            news = []
-            for k in range(9):
-                product = grad * band_rows[k, pl.ds(8, 32), :] * smooth[c, x, pl.ds(4 + k, 32), :]
-                news.append(sums9[k] + fold(product))
-            return tuple(news)
-
-        def class_body(step, sums4):
-            news = list(sums4)
-            for xl in range(2):
-                hidden = hid[c, 2 * source(step) + xl]
-                errors = errors_at(step, xl)
-                for k in range(4):
-                    news[k] = news[k] + fold(errors[k] * hidden)
-            return tuple(news)
-
-        sums9 = lax.fori_loop(
-            0, xs, wall_body, tuple(jnp.zeros((8, 128), F32) for k in range(9)), unroll=2
-        )
-        sums4 = lax.fori_loop(
-            0, size, class_body, tuple(jnp.zeros((8, 128), F32) for k in range(4)), unroll=2
-        )
-        for q, value in enumerate(sums25 + sums9 + sums4):
+        for q in range(38):
+            value = sums25[q] if q < 25 else acc[c, q - 25]
             red[pl.ds(q, 1), :] = jnp.sum(value, axis=0, keepdims=True)
         line = lax.dot_general(
             jnp.ones((8, 128), F32), red[...], (((1,), (1,)), ((), ())),
@@ -495,6 +500,7 @@
             pltpu.VMEM((size, cpg, 64, 128), BF16),
             pltpu.VMEM((size, 64, 128), F32),
             pltpu.VMEM((cpg, 9, 32, 128), F32),
+            pltpu.VMEM((cpg, 13, 8, 128), F32),
             pltpu.VMEM((128, 128), F32),
             pltpu.VMEM((everyone, 8, 128), F32),
             dma((chunks, size)), dma((chunks, size)), dma(()),

time: 70.5 us -> 70.1 us (level)
  no operation moved by 1% of the time
where the time goes in v4:
time: 70.1 us; the launch traced here: 69.7 us
  Pallas kernels  62.4 us (89%)
  local copies, waits for them, and re-layouts  5.72 us (8%)
  matrix products  0.87 us (1%)
    pallas_call x1, Pallas kernels, shards(): pl.pallas_call(functools.partial(kernel, (size, depth, cpg, chunks, volum...  62.4 us
    unnamed x16, local copies, waits for them, and re-layouts  5.72 us

profile of v4, /device:TPU:0, one launch (start us, length us, event | category | flops | bytes accessed | tf_op | source)
XLA Modules:
  0.0 69.7 jit_solution(13843679765428799419)
XLA Ops:
  0.6 0.0 copy-start
  0.6 0.0 copy-start.2
  0.7 0.7 copy-done
  1.3 0.0 copy-start.5
  1.3 0.9 %fusion.bands = f32[64,9]{1,0:T(8,128)S(1)} fusion(f32[16,9]{1,0:T(8,128)S(1)} %copy-done, s32[64]{0:T(128)} %param.9), kind=kOutput, calls=%fused_computation.1 | convolution fusion | flops 111616 | bytes 3136 | tf_op jit(solution)/shard_map/dot_general | solution.py:465
  2.2 0.0 copy-done.2
  2.2 0.0 copy-done.5
  2.2 0.0 copy-start.1
  2.2 1.0 %copy-done.1 = bf16[32,32,2,128]{3,2,1,0:T(2,128)(2,1)S(1)} copy-done((bf16[32,32,2,128]{3,2,1,0:T(2,128)(2,1)S(1)}, bf16[32,32,2,128]{3,2,1,0:T(2,128)(2,1)}, u32[]{:S(2)}) %copy-start.1) | copy-done | bytes 524312
  3.3 0.0 copy-start.3
  3.3 0.7 %copy-done.3 = f32[32,25]{1,0:T(8,128)S(1)} copy-done((f32[32,25]{1,0:T(8,128)S(1)}, f32[32,25]{1,0:T(8,128)}, u32[]{:S(2)}) %copy-start.3) | copy-done | bytes 3224
  4.0 0.0 copy-start.4
  4.0 0.7 copy-done.4
  4.7 62.4 %shard_map.102 = (bf16[32,64,128]{2,1,0:T(8,128)(2,1)S(1)}, f32[32,25]{1,0:T(8,128)S(1)}, f32[9,32]{1,0:T(8,128)S(1)}, f32[4,32]{1,0:T(4,128)S(1)}) custom-call(bf16[32,64,128]{2,1,0:T(8,128)(2,1)S(1)} %bitcast.6, s32[128,128]{1,0:T(8,128)S(1)} %bitcast.8, f32[64,9]{1,0:T(8,128)S(1)} %fusion.bands, f32[32,25]{1,0:T(8,128)S(1)} %copy-done.3, ...), custom_call_target="tpu_custom_call" | custom-call | tf_op jit(solution)/shard_map/pallas_call | solution.py:469
  67.1 0.8 %copy.17 = bf16[32,32,2,128]{3,2,1,0:T(2,128)(2,1)} copy(bf16[32,32,2,128]{3,2,1,0:T(2,128)(2,1)S(1)} %bitcast.7) | data formatting | bytes 1048576
  67.9 0.6 copy.18
  68.5 0.6 copy.19
  69.1 0.6 copy.20
Async XLA Ops:
  0.6 0.7 %copy-start = (f32[16,9]{1,0:T(8,128)S(1)}, f32[16,9]{1,0:T(8,128)}, u32[]{:S(2)}) copy-start(f32[16,9]{1,0:T(8,128)} %param.10) | copy-start | bytes 1732
  0.6 1.6 %copy-start.2 = (s32[64,2,128]{2,1,0:T(2,128)S(1)}, s32[64,2,128]{2,1,0:T(2,128)}, u32[]{:S(2)}) copy-start(s32[64,2,128]{2,1,0:T(2,128)} %param.8) | copy-start | bytes 196612
  1.3 0.9 %copy-start.5 = (f32[4,32]{1,0:T(4,128)S(1)}, f32[4,32]{1,0:T(4,128)}, u32[]{:S(2)}) copy-start(f32[4,32]{1,0:T(4,128)} %class_w.1) | copy-start | bytes 1540
  2.2 1.0 %copy-start.1 = (bf16[32,32,2,128]{3,2,1,0:T(2,128)(2,1)S(1)}, bf16[32,32,2,128]{3,2,1,0:T(2,128)(2,1)}, u32[]{:S(2)}) copy-start(bf16[32,32,2,128]{3,2,1,0:T(2,128)(2,1)} %param.7) | copy-start | bytes 1572868
  3.3 0.7 %copy-start.3 = (f32[32,25]{1,0:T(8,128)S(1)}, f32[32,25]{1,0:T(8,128)}, u32[]{:S(2)}) copy-start(f32[32,25]{1,0:T(8,128)} %tile_w.1) | copy-start | bytes 9604
  4.0 0.7 %copy-start.4 = (f32[32,9]{0,1:T(8,128)S(1)}, f32[32,9]{0,1:T(8,128)}, u32[]{:S(2)}) copy-start(f32[32,9]{0,1:T(8,128)} %param.12) | copy-start | bytes 3460
